TPU v7x, 768 devices: a whole 4x8x12 slice. The times are simulated.
768 devices in a mesh: dp: 32 (over y, z_hi, core), mp: 24 (over z_lo, x).
Axes of the slice: x: 4, y: 8, z: 12 (z_hi: 2, z_lo: 6; z = z_hi * 6 + z_lo), core: 2. Of those that a mesh axis runs over, the one named last changes fastest.
Arguments:
- patches: bfloat16 [4160, 1152, 256], P('dp', 'mp'), may hold values from -6 to 6
- picked: int32 [416], replicated, may hold values from 0 to 4159, as said below
- text_embed: bfloat16 [416, 1152], P('dp'), may hold values from -400 to 400
- weight_in: bfloat16 [1152, 2304], P(None, 'mp'), may hold values from -0.1875 to 0.1875
- weight_out: bfloat16 [2304, 1152], P('mp'), may hold values from -0.125 to 0.125
- logit_scale: float32 [1], replicated, may hold values from 3 to 8
- logit_bias: float32 [1], replicated, may hold values from -4 to -1
Outputs:
- embed_grad: float32 [416, 1152], P('dp')
Inputs may be any that keep to these rules, and one draw needn't show every extreme that they name: `picked`: entries are distinct super-batch indices; entries d*13 to (d+1)*13 - 1 belong to learner d; of them at most 2 lie in one source block of 130 consecutive indices, and exactly 2 do for some source in every learner's list.
All inputs are finite; a program needn't handle non-finite values.
Results may differ from a plain program's by a relative error of at most 0.00075.
Values may be sent and summed in bfloat16 or wider, within the bound.
A program may use at most 64 MiB of HBM per device.

v0:
```python
import jax
import jax.numpy as jnp
from jax import lax
from jax.sharding import PartitionSpec as P

CAP = 2


layer_eps = 1e-06


def normalize_middle(values_bf):
    values = values_bf.astype(jnp.float32)
    center = jnp.mean(values, axis=1, keepdims=True)
    spread = jnp.mean((values - center) ** 2, axis=1, keepdims=True)
    return ((values - center) * lax.rsqrt(spread + layer_eps)).astype(jnp.bfloat16)


def body(patches, picked, text_embed, weight_in, weight_out, logit_scale, logit_bias):
    dp_ranks = lax.axis_size("dp")
    my_rank = lax.axis_index("dp")
    super_rows = patches.shape[0]
    feat_cols = patches.shape[1]
    npatch = patches.shape[2]
    images = picked.shape[0] // dp_ranks
    lists = picked.reshape(dp_ranks, images)
    source = lists // super_rows
    mine = (source == my_rank).astype(jnp.int32)
    slot_of = jnp.cumsum(mine, axis=1) - mine
    local_idx = lists % super_rows
    capacity = CAP
    onehot = mine[:, :, None] * (
        slot_of[:, :, None] == jnp.arange(capacity, dtype=jnp.int32)[None, None, :]
    ).astype(jnp.int32)
    send_idx = jnp.sum(onehot * local_idx[:, :, None], axis=1)
    filled = jnp.sum(onehot, axis=1).astype(jnp.bfloat16)
    outgoing = patches[send_idx.reshape(-1)] * filled.reshape(-1)[:, None, None]
    outgoing = outgoing.reshape(dp_ranks, capacity, feat_cols, npatch)
    arrived = lax.all_to_all(outgoing, "dp", split_axis=0, concat_axis=0, tiled=True)
    own_list = lax.dynamic_index_in_dim(lists, my_rank, 0, keepdims=False)
    own_src = own_list // super_rows
    order_ids = jnp.arange(images, dtype=jnp.int32)
    same_src = own_src[:, None] == own_src[None, :]
    earlier = order_ids[:, None] > order_ids[None, :]
    own_slot = jnp.sum((same_src & earlier).astype(jnp.int32), axis=1)
    received = arrived.reshape(dp_ranks * capacity, feat_cols, npatch)[
        own_src * capacity + own_slot
    ]
    gathered = lax.all_gather(received, "mp", axis=1, tiled=True)
    normed = normalize_middle(gathered)
    hidden = jax.nn.gelu(
        jnp.einsum("idp,df->ipf", normed, weight_in, preferred_element_type=jnp.float32),
        approximate=True,
    )
    pooled = jnp.mean(hidden, axis=1).astype(jnp.bfloat16)
    partial_value = jnp.dot(pooled, weight_out, preferred_element_type=jnp.float32)
    row_mean = jnp.mean(received, axis=2, dtype=jnp.float32)
    col_start = lax.axis_index("mp") * feat_cols
    current = lax.dynamic_slice(partial_value, (0, col_start), (images, feat_cols))
    partial_value = lax.dynamic_update_slice(partial_value, current + row_mean, (0, col_start))
    embed = lax.psum(partial_value, "mp")
    length = jnp.sqrt(jnp.sum(embed * embed, axis=-1, keepdims=True) + layer_eps)
    unit = embed / length
    scale = logit_scale[0]
    bias = logit_bias[0]
    global_rows = my_rank * images + jnp.arange(images, dtype=jnp.int32)
    block_text = lax.all_gather(text_embed, "dp", axis=0, tiled=True)
    text_vals = block_text.astype(jnp.float32)
    text_unit = text_vals / jnp.sqrt(
        jnp.sum(text_vals * text_vals, axis=-1, keepdims=True) + layer_eps
    )
    logits = scale * jnp.dot(unit, text_unit.T, precision=lax.Precision.HIGHEST) + bias
    global_cols = jnp.arange(block_text.shape[0], dtype=jnp.int32)
    label = jnp.where(global_rows[:, None] == global_cols[None, :], 1.0, -1.0).astype(jnp.float32)
    slope = -label * jax.nn.sigmoid(-label * logits)
    summed = jnp.dot(slope, text_unit, precision=lax.Precision.HIGHEST)
    unit_grad = scale * summed
    along = jnp.sum(unit * unit_grad, axis=-1, keepdims=True)
    return (unit_grad - unit * along) / length


def solution(mesh):
    in_specs = (P("dp", "mp", None), P(), P("dp", None), P(None, "mp"), P("mp", None), P(), P())
    out_specs = P("dp", None)
    return jax.shard_map(body, mesh=mesh, in_specs=in_specs, out_specs=out_specs, check_vma=False)
```

profile of v0, /device:TPU:56, one launch (start us, length us, event | category | flops | bytes accessed | tf_op | source)
XLA Modules:
  0.0 460.6 jit_solution(6256519342717667485)
XLA Ops:
  6.5 0.9 reshape.223
  7.6 0.2 reduce_window_sum.11
  8.3 0.1 copy-done
  8.5 1.8 gather_fusion
  10.3 2.7 broadcast_multiply_fusion
  13.0 19.9 %all-to-all-start = ((bf16[32,2,48,256]{3,2,1,0:T(8,128)(2,1)}), bf16[32,2,48,256]{3,2,1,0:T(8,128)(2,1)}, u32[]{:S(2)}, u32[]{:S(2)}) async-start(bf16[32,2,48,256]{3,2,1,0:T(8,128)(2,1)} %broadcast_multiply_fusion), calls=%async_computation | async-start | bytes 3145728 | tf_op jit(solution)/shard_map/all_to_all | solution.py:39
  33.0 0.2 convert_reduce_fusion.2
  33.2 40.6 %all-to-all-done = bf16[32,2,48,256]{3,2,1,0:T(8,128)(2,1)} async-done(((bf16[32,2,48,256]{3,2,1,0:T(8,128)(2,1)}), bf16[32,2,48,256]{3,2,1,0:T(8,128)(2,1)}, u32[]{:S(2)}, u32[]{:S(2)}) %all-to-all-start) | async-done | bytes 1572896 | tf_op jit(solution)/shard_map/all_to_all | solution.py:39
  73.8 2.7 gather_fusion.1
  76.6 85.7 %all-gather.1 = bf16[32,13,1152]{2,1,0:T(8,128)(2,1)} all-gather(bf16[1,13,1152]{2,1,0:T(8,128)(2,1)S(1)} %bitcast.40), channel_id=1, replica_groups=mesh['dp'=32,'mp'=24] {'dp'}, dimensions={0}, use_global_device_ids=true | all-gather | bytes 988416 | tf_op jit(solution)/shard_map/all_gather | solution.py:67
  162.3 2.6 reshape.245
  166.2 1.7 multiply_reduce_fusion
  167.9 0.2 convert_reduce_fusion.1
  168.1 114.7 %all-gather.4.cloned.1.call-done = bf16[13,1152,256]{2,1,0:T(8,128)(2,1)} async-done(((bf16[13,48,256]{2,1,0:T(8,128)(2,1)}), bf16[13,1152,256]{2,1,0:T(8,128)(2,1)}) %all-gather.4.cloned.1.call-update) | async-done | bytes 7667728 | tf_op jit(solution)/shard_map/all_gather | solution.py:49
  282.8 4.3 convert_reduce_fusion
  287.2 1.0 copy-done.1
  288.2 2.0 fusion.2
  290.2 2.6 fusion.15
  292.8 0.1 fusion.31
  293.1 0.2 dynamic_update_slice.3
  293.3 154.8 %psum.7 = f32[13,1152]{1,0:T(8,128)S(1)} all-reduce(f32[13,1152]{1,0:T(8,128)S(1)} %dynamic_update_slice.3), channel_id=1, replica_groups=mesh['dp'=32,'mp'=24] {'mp'}, use_global_device_ids=true, to_apply=%region_8.9 | all-reduce | flops 14976 | bytes 119808 | tf_op jit(solution)/shard_map/psum | solution.py:61
  448.3 3.5 fusion.22
  451.8 1.3 multiply_reduce_fusion.1
  453.1 0.7 subtract_divide_fusion
  (38 shorter events, 1.0 us)
Async XLA Ops:
  6.5 1.9 copy-start
  13.0 63.6 %copy-start.5 = (bf16[13,1152]{1,0:T(8,128)(2,1)S(1)}, bf16[13,1152]{1,0:T(8,128)(2,1)}, u32[]{:S(2)}) copy-start(bf16[13,1152]{1,0:T(8,128)(2,1)} %param.9) | copy-start | bytes 89860
  13.0 60.8 %all-to-all-start = ((bf16[32,2,48,256]{3,2,1,0:T(8,128)(2,1)}), bf16[32,2,48,256]{3,2,1,0:T(8,128)(2,1)}, u32[]{:S(2)}, u32[]{:S(2)}) async-start(bf16[32,2,48,256]{3,2,1,0:T(8,128)(2,1)} %broadcast_multiply_fusion), calls=%async_computation | async-start | bytes 3145728 | tf_op jit(solution)/shard_map/all_to_all | solution.py:39
  32.9 249.9 %all-gather.4.cloned.1.call-start = ((), (), s32[]{:S(2)}) async-start(), calls=%async_computation.1 | async-start | bytes 7987200 | tf_op jit(solution)/shard_map/all_gather | solution.py:49
  162.3 5.7 %copy-start.3 = (bf16[13,48,256]{2,1,0:T(8,128)(2,1)S(1)}, bf16[13,48,256]{2,1,0:T(8,128)(2,1)}, u32[]{:S(2)}) copy-start(bf16[13,48,256]{2,1,0:T(8,128)(2,1)} %gather_fusion.1) | copy-start | bytes 958468
  282.8 5.4 %copy-start.1 = (bf16[13,1152,256]{2,1,0:T(8,128)(2,1)S(1)}, bf16[13,1152,256]{2,1,0:T(8,128)(2,1)}, u32[]{:S(2)}) copy-start(bf16[13,1152,256]{2,1,0:T(8,128)(2,1)} %all-gather.4.cloned.1.call-done) | copy-start | bytes 23003140
  288.2 2.0 copy-start.6
  290.2 2.6 copy-start.4
  448.3 3.5 copy-start.2
Sparse Core Ops, SparseCore 0:
  76.7 206.1 all-gather.3
where the time goes:
time: 461 us
  blocking collectives  241 us (52%)
  waiting for transfers between devices  155 us (34%)
  starting transfers between devices  20 us (4%)
  between operations  14.9 us (3%)
  other arithmetic  12.4 us (3%)
  local copies, waits for them, and re-layouts  9.97 us (2%)
  matrix products  7.52 us (2%)
    psum x1, blocking collectives, body(): embed = lax.psum(partial_value, 'mp')  155 us
    all_gather x1, waiting for transfers between devices, body(): gathered = lax.all_gather(received, 'mp', axis=1, tiled=True)  115 us
    all_gather x1, blocking collectives, body(): block_text = lax.all_gather(text_embed, 'dp', axis=0, tiled=True)  85.7 us
    all_to_all x1, waiting for transfers between devices, body(): lax.all_to_all(outgoing, 'dp', split_axis=0, concat_axis=0, tiled=True)  40.6 us
    all_to_all x1, starting transfers between devices, body(): lax.all_to_all(outgoing, 'dp', split_axis=0, concat_axis=0, tiled=True)  19.9 us
  transfers between devices with their start and end apart: 2, of which 2 were waited for; matrix products, arithmetic and copies ran while one was open for 1% of the time, Pallas kernels for 0%

commit v1 on v0

v1 whole, which is shorter than its diff:
```python
import jax
import jax.numpy as jnp
from jax import lax
from jax.experimental import pallas as pl
from jax.experimental.pallas import tpu as pltpu
from jax.sharding import PartitionSpec as P

MESH = pl.DeviceIdType.MESH
F32, BF16 = jnp.float32, jnp.bfloat16
EPS = 1e-06
NY, NH, NC, NQ, NX = 8, 2, 2, 6, 4
NZ = NH * NQ
NS = NY * NC
IMG = 13
SUP = 130
FEAT, NP = 48, 256
D, HID = 1152, 576
ROWS, LANES = 16, 128
NF, NPC = FEAT // ROWS, NP // LANES
CH = NF * NPC
AHEAD = 3
EXTRA = 2
NT = (((1,), (1,)), ((), ()))


def split3(v):
    hi = v.astype(BF16)
    rest = v - hi.astype(F32)
    mid = rest.astype(BF16)
    lo = (rest - mid.astype(F32)).astype(BF16)
    return jnp.concatenate([hi, mid, lo], axis=0)


def sum3(v):
    n = v.shape[0] // 3
    return (v[2 * n :] + v[n : 2 * n]) + v[:n]


def row_ones(r, width, value, dtype):
    rows = lax.broadcasted_iota(jnp.int32, (8, width), 0)
    return jnp.where(rows == r, F32(value), F32(0.0)).astype(dtype)


def kernel(*refs):
    (patches, send_idx, comp_idx, half_idx, text, w_in, w_out, scale_ref, bias_ref, out) = refs[:10]
    refs = refs[10:]
    pv, wv, ys, zs, xb, wb, tb, normed, acc, pooled, mean_rows, f1, f2, itl = refs[:14]
    yr = refs[14 : 14 + CH]
    zr = refs[14 + CH : 14 + 2 * CH]
    (lsem, ysend, yrecv, zsend, zrecv, zxsend, zxrecv, xsend, xrecv, wsend, wrecv, dsend, drecv,
     tsend, trecv, f1send, f1recv, f2send, f2recv) = refs[14 + 2 * CH :]

    dp = lax.axis_index("dp")
    mp = lax.axis_index("mp")
    y, h, c = dp // 4, (dp // 2) % 2, dp % 2
    q, x = mp // NX, mp % NX
    z = h * NQ + q
    me = y * NC + c

    def ydev(s):
        return (((s // 2) * 2 + h) * 2 + s % 2, mp)

    def zdev(t):
        return ((y * 2 + t // NQ) * 2 + c, (t % NQ) * NX + x)

    def xdev(k):
        return (dp, q * NX + k)

    def core_dev():
        return (y * 4 + h * 2 + 1 - c, mp)

    def remote(src, dst, ssem, rsem, dev):
        return pltpu.make_async_remote_copy(
            src_ref=src, dst_ref=dst, send_sem=ssem, recv_sem=rsem, device_id=dev, device_id_type=MESH)

    def wait(ref, sem):
        pltpu.make_async_copy(ref, ref, sem).wait()

    load_p = pltpu.make_async_copy(patches, pv, lsem.at[0])
    load_p.start()
    load_i = pltpu.make_async_copy(w_in, wv, lsem.at[1])
    load_i.start()
    load_o = pltpu.make_async_copy(w_out, wb.at[1, q], lsem.at[2])
    load_o.start()

    barrier = pltpu.get_barrier_semaphore()

    def greet(dev):
        pl.semaphore_signal(barrier, inc=1, device_id=dev, device_id_type=MESH)

    @pl.loop(1, NS)
    def _(o):
        greet(ydev((me + o) % NS))

    @pl.loop(1, NZ)
    def _(o):
        greet(zdev((z + o) % NZ))

    @pl.loop(1, NX)
    def _(o):
        greet(xdev((x + o) % NX))

    @pl.when(y // 2 == x)
    def _():
        tb[c, h, y] = jnp.concatenate([text[...].astype(F32), jnp.zeros((ROWS - IMG, D), F32)], axis=0).astype(BF16)

    def gather(k):
        pc, fc = k // NF, k % NF

        @pl.loop(0, NS * 4, unroll=8)
        def _(s):
            image = pv[send_idx[s], fc * ROWS : (fc + 1) * ROWS, pc * LANES : (pc + 1) * LANES]
            ys[k, s // 4, s % 4] = image

        yr[k][pl.ds(me * 4, 4)] = ys[k, me]

    def start_y(k):
        @pl.loop(1, NS)
        def _(o):
            s = (me + o) % NS
            remote(ys.at[k, s], yr[k].at[pl.ds(me * 4, 4)], ysend.at[k], yrecv.at[k], ydev(s)).start()

    load_p.wait()
    gather(0)
    pl.semaphore_wait(barrier, NS - 1 + NZ - 1 + NX - 1)
    start_y(0)
    load_i.wait()
    load_o.wait()
    rows = lax.broadcasted_iota(jnp.int32, (96, 96), 0)
    cols = lax.broadcasted_iota(jnp.int32, (96, 96), 1)
    eye = jnp.where(rows == cols, F32(1.0), F32(0.0)).astype(BF16)
    wb[0, q] = lax.dot_general(eye, wv[...], NT, preferred_element_type=F32).astype(BF16)

    up, down = (z + 1) % NZ, (z + NZ - 1) % NZ

    def qq(k):
        return (q + k + NQ) % NQ

    def w_piece(rnd, way):
        k = qq(-rnd if way == 0 else rnd)
        if rnd == 2:
            return wb.at[c, k, pl.ds(0 if way == 0 else 48, 48)]
        return wb.at[c, k]

    def w_copy(rnd, way):
        piece = w_piece(rnd, way)
        return remote(piece, piece, wsend.at[rnd, way], wrecv.at[rnd, way], zdev(up if way == 0 else down))

    def w_start(rnd):
        w_copy(rnd, 0).start()
        w_copy(rnd, 1).start()

    def w_wait(rnd):
        w_copy(rnd, 0).wait_recv()
        w_copy(rnd, 1).wait_recv()

    def d_copy(j):
        k = (qq(-1), qq(1), qq(-2), qq(2), qq(3))[j]
        return remote(wb.at[c, k], wb.at[c, k], dsend.at[j], drecv.at[j], core_dev())

    w_start(0)
    gather(1)
    start_y(1)

    @pl.when(y // 2 == x)
    def _():
        @pl.loop(1, NY)
        def _(o):
            to = (y + o) % NY
            remote(tb.at[c, h, y], tb.at[c, h, y], tsend.at[0], trecv.at[y % 2], ((to * 2 + h) * 2 + c, mp)).start()

    gather(2)
    start_y(2)

    def t_mirror():
        piece = tb.at[c, h, pl.ds(2 * x, 2)]
        return remote(piece, piece, tsend.at[1], trecv.at[2], zdev(NZ - 1 - z))

    def t_gather(k):
        piece = tb.at[c, :, pl.ds(2 * x, 2)]
        return remote(piece, piece, tsend.at[2], trecv.at[3 + x], xdev(k))

    def t_core():
        return remote(tb.at[c], tb.at[c], tsend.at[3], trecv.at[7], core_dev())

    def compact(k):
        @pl.loop(0, NZ * 3, unroll=6)
        def _(g):
            zs[k, g // 3, g % 3] = yr[k][comp_idx[g]]

        zr[k][z] = zs[k, z]

    def start_z(k):
        @pl.loop(1, NZ)
        def _(o):
            t = (z + o) % NZ
            remote(zs.at[k, t, pl.ds(0, 2)], zr[k].at[z, pl.ds(0, 2)], zsend.at[k], zrecv.at[k], zdev(t)).start()

        for e in range(NH):
            t = e * NQ + EXTRA

            @pl.when(z != t)
            def _():
                remote(zs.at[k, t, pl.ds(2, 1)], zr[k].at[z, pl.ds(2, 1)], zxsend.at[k, e], zxrecv.at[k], zdev(t)).start()

    extra = q == EXTRA

    def wait_z(k):
        wait(zr[k].at[pl.ds(0, NZ - 1), pl.ds(0, 2)], zrecv.at[k])

        @pl.when(extra)
        def _():
            wait(zr[k].at[pl.ds(0, NZ - 1), pl.ds(2, 1)], zxrecv.at[k])

    def select(k):
        pc, fc = k // NF, k % NF

        @pl.loop(0, NQ)
        def _(s):
            for r in range(2):
                xb[pc, r, s, x, fc] = zr[k][half_idx[r] + s, r]

        @pl.when(extra)
        def _():
            @pl.loop(0, NQ)
            def _(s):
                xb[pc, 2, s, x, fc] = zr[k][half_idx[2] + s, 2]

    def x_piece(k, r0, n, owner):
        return xb.at[k // NF, pl.ds(r0, n), :, owner, k % NF]

    def x_copy(k, r0, n, owner, to):
        piece = x_piece(k, r0, n, owner)
        i = 0 if r0 == 0 else 1
        return remote(piece, piece, xsend.at[k, i, to], xrecv.at[k, i, owner], xdev(to))

    def start_x(k):
        @pl.loop(1, NX)
        def _(o):
            x_copy(k, 0, 2, x, (x + o) % NX).start()

        @pl.when(extra)
        def _():
            @pl.loop(1, NX)
            def _(o):
                x_copy(k, 2, 1, x, (x + o) % NX).start()

    def wait_x(k):
        @pl.loop(1, NX)
        def _(o):
            owner = (x + o) % NX
            wait(x_piece(k, 0, 2, owner), xrecv.at[k, 0, owner])

        @pl.when(extra)
        def _():
            @pl.loop(1, NX)
            def _(o):
                owner = (x + o) % NX
                wait(x_piece(k, 2, 1, owner), xrecv.at[k, 1, owner])

    def normalize(pc, r):
        flat = xb[pc, r].reshape(D, LANES)
        values = flat.astype(F32)
        center = jnp.sum(values, axis=0, keepdims=True) * F32(1.0 / D)
        values = values - center
        spread = jnp.sum(values * values, axis=0, keepdims=True) * F32(1.0 / D)
        mean = lax.dot_general(row_ones(r, LANES, 1.0 / (NP * NX), BF16), flat, NT, preferred_element_type=F32)
        mean_rows[...] += mean
        return (values * lax.rsqrt(spread + F32(EPS))).astype(BF16)

    def hidden(pc, lanes, first):
        weights = wb[0].reshape(HID, D)
        value = jnp.dot(weights, normed[:, lanes], preferred_element_type=F32)
        value = jax.nn.gelu(value, approximate=True)
        if pc == 0:
            acc[:, lanes] = value
        else:
            acc[:, lanes] += value

    def compute(pc):
        normed[:, 0:LANES] = normalize(pc, 0)
        normed[:, LANES : 2 * LANES] = normalize(pc, 1)
        hidden(pc, slice(0, 2 * LANES), 0)

        @pl.when(extra)
        def _():
            normed[:, 2 * LANES :] = normalize(pc, 2)
            hidden(pc, slice(2 * LANES, 3 * LANES), 2)

    def pool(r):
        total = acc[:, r * LANES : (r + 1) * LANES]
        pooled[...] += lax.dot_general(
            row_ones(r, LANES, 1.0 / NP, F32), total, NT, precision=lax.Precision.HIGHEST, preferred_element_type=F32)

    mean_rows[...] = jnp.zeros((8, D), F32)
    pooled[...] = jnp.zeros((8, HID), F32)

    for k in range(CH):
        wait(yr[k].at[pl.ds(0, (NS - 1) * 4)], yrecv.at[k])
        compact(k)
        start_z(k)
        if k + AHEAD < CH:
            gather(k + AHEAD)
            start_y(k + AHEAD)
        if k == 0:
            w_wait(0)
            w_start(1)
            d_copy(0).start()
            d_copy(1).start()
            for j in range(2):

                @pl.when(2 * x + j != y)
                def _():
                    wait(tb.at[c, h, 2 * x + j], trecv.at[j])

            t_mirror().start()
        elif k == 1:
            w_wait(1)
            w_start(2)
            d_copy(2).start()
            d_copy(3).start()
            t_mirror().wait_recv()

            @pl.loop(1, NX)
            def _(o):
                t_gather((x + o) % NX).start()
        elif k == 2:
            w_wait(2)
            d_copy(4).start()

            @pl.loop(1, NX)
            def _(o):
                owner = (x + o) % NX
                wait(tb.at[c, :, pl.ds(2 * owner, 2)], trecv.at[3 + owner])

            t_core().start()
        if k >= 1:
            wait_z(k - 1)
            select(k - 1)
            start_x(k - 1)
        if k == 4:
            for j in range(5):
                kk = (qq(-1), qq(1), qq(-2), qq(2), qq(3))[j]
                wait(wb.at[1 - c, kk], drecv.at[j])
            for j in range(NF):
                wait_x(j)
            compute(0)
    wait(tb.at[1 - c], trecv.at[7])
    squares = tb[...].reshape(NS * NH * ROWS, D).astype(F32)
    squares = squares * squares
    hi = squares.astype(BF16)
    lo = (squares - hi.astype(F32)).astype(BF16)
    ones = jnp.ones((8, D), BF16)
    total = lax.dot_general(ones, lo, NT, preferred_element_type=F32)
    total = total + lax.dot_general(ones, hi, NT, preferred_element_type=F32)
    itl[...] = 1.0 / jnp.sqrt(total + F32(EPS))

    wait_z(CH - 1)
    select(CH - 1)
    start_x(CH - 1)
    for j in range(NF, CH):
        wait_x(j)
    compute(1)
    pool(0)
    pool(1)

    @pl.when(extra)
    def _():
        pool(2)

    embed = jnp.dot(pooled[...].astype(BF16), wb[1].reshape(HID, D), preferred_element_type=F32)
    f1[x] = embed + mean_rows[...]

    def f1_copy(owner, to):
        return remote(f1.at[owner], f1.at[owner], f1send.at[to], f1recv.at[owner], xdev(to))

    @pl.loop(1, NX)
    def _(o):
        f1_copy(x, (x + o) % NX).start()

    @pl.loop(1, NX)
    def _(o):
        owner = (x + o) % NX
        wait(f1.at[owner], f1recv.at[owner])

    f2[q] = (f1[0] + f1[1]) + (f1[2] + f1[3])

    def f2_copy(owner, to):
        return remote(f2.at[owner], f2.at[owner], f2send.at[to], f2recv.at[owner], (dp, to * NX + x))

    @pl.loop(1, NQ)
    def _(o):
        f2_copy(q, (q + o) % NQ).start()

    @pl.loop(1, NQ)
    def _(o):
        owner = (q + o) % NQ
        wait(f2.at[owner], f2recv.at[owner])

    plane = f2[...]
    embed = jnp.concatenate(
        [plane[k, 0:2] for k in range(NQ)] + [plane[EXTRA, 2:3], jnp.zeros((ROWS - IMG, D), F32)], axis=0)
    length = jnp.sqrt(jnp.sum(embed * embed, axis=1, keepdims=True) + F32(EPS))
    unit = embed / length
    scale = scale_ref[0]
    table = tb[...].reshape(NS * NH * ROWS, D)
    dots = sum3(lax.dot_general(split3(unit), table, NT, preferred_element_type=F32))
    inverse = itl[0:1, :]
    logits = scale * (dots * inverse) + bias_ref[0]
    row = lax.broadcasted_iota(jnp.int32, logits.shape, 0)
    col = lax.broadcasted_iota(jnp.int32, logits.shape, 1)
    label = jnp.where(col == ((c * NH + h) * NY + y) * ROWS + row, F32(1.0), F32(-1.0))
    slope = -label * jax.nn.sigmoid(-label * logits)
    summed = sum3(jnp.dot(split3(slope * inverse), table, preferred_element_type=F32))
    unit_grad = scale * summed
    along = jnp.sum(unit * unit_grad, axis=1, keepdims=True)
    out[...] = ((unit_grad - unit * along) / length)[0:IMG]

    for k in range(CH):
        wait(yr[k].at[pl.ds(0, (NS - 1) * 4)], ysend.at[k])
        wait(zs.at[k, pl.ds(0, NZ - 1), pl.ds(0, 2)], zsend.at[k])
        for e in range(NH):
            t = e * NQ + EXTRA

            @pl.when(z != t)
            def _():
                wait(zs.at[k, t, pl.ds(2, 1)], zxsend.at[k, e])

        @pl.loop(1, NX)
        def _(o):
            x_copy(k, 0, 2, x, (x + o) % NX).wait_send()

        @pl.when(extra)
        def _():
            @pl.loop(1, NX)
            def _(o):
                x_copy(k, 2, 1, x, (x + o) % NX).wait_send()

    for rnd in range(3):
        w_copy(rnd, 0).wait_send()
        w_copy(rnd, 1).wait_send()
    for j in range(5):
        d_copy(j).wait_send()

    @pl.when(y // 2 == x)
    def _():
        wait(tb.at[c, h, pl.ds(0, NY - 1)], tsend.at[0])

    t_mirror().wait_send()
    wait(tb.at[pl.ds(0, 1), :, pl.ds(0, 6)], tsend.at[2])
    t_core().wait_send()

    @pl.loop(1, NX)
    def _(o):
        f1_copy(x, (x + o) % NX).wait_send()

    @pl.loop(1, NQ)
    def _(o):
        f2_copy(q, (q + o) % NQ).wait_send()


def body(patches, picked, text_embed, weight_in, weight_out, logit_scale, logit_bias):
    dp = lax.axis_index("dp")
    y, h, c = dp // 4, (dp // 2) % 2, dp % 2
    q = lax.axis_index("mp") // NX
    i32 = jnp.int32
    lists = picked.reshape(32, IMG)
    source = lists // SUP
    local = lists - source * SUP
    order = jnp.arange(IMG, dtype=i32)
    same = (source[:, :, None] == source[:, None, :]) & (order[:, None] > order[None, :])[None]
    slot = jnp.sum(same.astype(i32), axis=2)
    mine = source == dp
    send_idx = jnp.stack([jnp.sum(jnp.where(mine & (slot == k), local, 0), axis=1) for k in range(2)], axis=1)
    send_idx = send_idx.reshape(NY, NH, NC, 2).transpose(0, 2, 1, 3).reshape(NS * 4)

    def pair(a):
        return jnp.take(a.reshape(NY, NH, NC, IMG), y, axis=0)[:, c]

    src, slots = pair(source), pair(slot)
    src_half = (src // 2) % 2
    flat = ((src // 4) * 2 + src % 2) * 4 + jnp.arange(NH, dtype=i32)[:, None] * 2 + slots
    flat = jnp.where(src_half == h, flat, 0)
    last = jnp.broadcast_to(flat[:, None, IMG - 1 :], (NH, NQ, 1))
    comp_idx = jnp.concatenate([flat[:, : IMG - 1].reshape(NH, NQ, 2), last], axis=2).reshape(NZ * 3)
    own = jnp.take(src_half, h, axis=0)
    half_idx = NQ * jnp.concatenate([lax.dynamic_slice(own, (2 * q,), (2,)), own[IMG - 1 :]])

    smem = pl.BlockSpec(memory_space=pltpu.SMEM)
    hbm = pl.BlockSpec(memory_space=pl.ANY)
    vmem = pl.BlockSpec(memory_space=pltpu.VMEM)
    dma = pltpu.SemaphoreType.DMA
    return pl.pallas_call(
        kernel,
        out_shape=jax.ShapeDtypeStruct((IMG, D), F32),
        in_specs=[hbm, smem, smem, smem, vmem, hbm, hbm, smem, smem],
        out_specs=vmem,
        scratch_shapes=[
            pltpu.VMEM((SUP, FEAT, NP), BF16),
            pltpu.VMEM((D, 96), BF16),
            pltpu.VMEM((CH, NS, 4, ROWS, LANES), BF16),
            pltpu.VMEM((CH, NZ, 3, ROWS, LANES), BF16),
            pltpu.VMEM((NPC, 3, NQ, NX, NF, ROWS, LANES), BF16),
            pltpu.VMEM((2, NQ, 96, D), BF16),
            pltpu.VMEM((NC, NH, NY, ROWS, D), BF16),
            pltpu.VMEM((D, 3 * LANES), BF16),
            pltpu.VMEM((HID, 3 * LANES), F32),
            pltpu.VMEM((8, HID), F32),
            pltpu.VMEM((8, D), F32),
            pltpu.VMEM((NX, 8, D), F32),
            pltpu.VMEM((NQ, 8, D), F32),
            pltpu.VMEM((8, NS * NH * ROWS), F32),
        ]
        + [pltpu.VMEM((NS * 4, ROWS, LANES), BF16)] * CH
        + [pltpu.VMEM((NZ, 3, ROWS, LANES), BF16)] * CH
        + [
            dma((3,)), dma((CH,)), dma((CH,)), dma((CH,)), dma((CH,)), dma((CH, NH)), dma((CH,)),
            dma((CH, 2, NX)), dma((CH, 2, NX)), dma((3, 2)), dma((3, 2)), dma((5,)), dma((5,)),
            dma((4,)), dma((8,)), dma((NX,)), dma((NX,)), dma((NQ,)), dma((NQ,)),
        ],
        compiler_params=pltpu.CompilerParams(
            collective_id=0, has_side_effects=True, vmem_limit_bytes=50 * 1024 * 1024),
        cost_estimate=pl.CostEstimate(flops=2_000_000_000, bytes_accessed=5_000_000, transcendentals=1_000_000),
    )(patches, send_idx.astype(i32), comp_idx.astype(i32), half_idx.astype(i32), text_embed, weight_in, weight_out,
      logit_scale, logit_bias)


def solution(mesh):
    in_specs = (P("dp", "mp", None), P(), P("dp", None), P(None, "mp"), P("mp", None), P(), P())
    return jax.shard_map(body, mesh=mesh, in_specs=in_specs, out_specs=P("dp", None), check_vma=False)
```

time: 461 us -> 107 us (0.23)
  the two profiles are of different devices: /device:TPU:56 before, /device:TPU:40 now
where the time goes in v1:
time: 107 us
  Pallas kernels  94.7 us (89%)
  local copies, waits for them, and re-layouts  8.25 us (8%)
  other arithmetic  2.46 us (2%)
  between operations  1.41 us (1%)
    pallas_call x1, Pallas kernels, body(): pl.pallas_call(kernel, out_shape=jax.ShapeDtypeStruct((IMG, D), F32), in_...  94.7 us
    unnamed x8, local copies, waits for them, and re-layouts  5.39 us

profile of v1, /device:TPU:40, one launch (start us, length us, event | category | flops | bytes accessed | tf_op | source)
XLA Modules:
  0.0 106.8 jit_solution(6418734451383367951)
XLA Ops:
  1.3 0.7 fusion.3
  2.0 0.7 broadcast_divide_fusion
  2.7 0.1 and.86
  2.8 0.1 div.62
  2.9 0.8 reshape.90
  3.7 0.1 copy.27
  3.8 0.1 convert_reduce_fusion
  4.0 0.1 stack.9
  4.1 0.1 copy.31
  4.2 0.1 stack.10
  4.3 0.1 copy.32
  4.4 0.1 copy.34
  4.6 0.6 slice.30
  5.3 0.7 add_multiply_fusion.refs_3_
  6.0 0.2 slice_reduce_fusion
  6.4 0.1 reshape.94.refs_2_
  6.5 0.1 copy.33
  6.6 0.1 reshape.91.refs_1_
  6.7 1.1 %copy.35.refs_5_ = bf16[1152,96]{1,0:T(8,128)(2,1)S(1)} copy(bf16[1152,96]{0,1:T(8,128)(2,1)} %param.12) | data formatting | bytes 442368 | tf_op args[3]
  7.9 1.9 %copy-done = bf16[130,48,256]{2,1,0:T(8,128)(2,1)S(1)} copy-done((bf16[130,48,256]{2,1,0:T(8,128)(2,1)S(1)}, bf16[130,48,256]{2,1,0:T(8,128)(2,1)}, u32[]{:S(2)}) %copy-start) | copy-done | bytes 3194904
  9.8 0.9 copy-done.1
  10.7 0.8 copy-done.2
  11.5 94.7 %shard_map.73 = f32[13,1152]{1,0:T(8,128)S(1)} custom-call(bf16[130,48,256]{2,1,0:T(8,128)(2,1)S(1)} %copy-done, s32[64]{0:T(128)S(1)} %reshape.91.refs_1_, s32[36]{0:T(128)S(1)} %reshape.94.refs_2_, s32[3]{0:T(128)S(1)} %add_multiply_fusion.refs_3_, bf16[13,1152]{1,0:T(8,128)(2,1)S(1)} %copy-done.2, bf16[1152,96]{1,0:T(8,128)(2,1)S(1)} %copy.35.refs_5_, ...), custom_call_target="tpu_custom_call" | custom-call | flops 2000000000 | bytes 5000000 | tf_op jit(solution)/shard_map/pallas_call | solution.py:493
  106.2 0.6 copy.39
  (17 shorter events, 0.5 us)
Async XLA Ops:
  7.9 1.9 %copy-start = (bf16[130,48,256]{2,1,0:T(8,128)(2,1)S(1)}, bf16[130,48,256]{2,1,0:T(8,128)(2,1)}, u32[]{:S(2)}) copy-start(bf16[130,48,256]{2,1,0:T(8,128)(2,1)} %refs_0_.1) | copy-start | bytes 9584644
  9.8 0.9 copy-start.1
  10.7 0.8 copy-start.2

commit v2 on v1

v2 whole, which is shorter than its diff:
```python
import jax
import jax.numpy as jnp
from jax import lax
from jax.experimental import pallas as pl
from jax.experimental.pallas import tpu as pltpu
from jax.sharding import PartitionSpec as P

MESH = pl.DeviceIdType.MESH
F32, BF16 = jnp.float32, jnp.bfloat16
EPS = 1e-06
NY, NH, NC, NQ, NX = 8, 2, 2, 6, 4
NZ = NH * NQ
NS = NY * NC
IMG = 13
SUP = 130
FEAT, NP = 48, 256
D, HID = 1152, 576
ROWS, LANES = 16, 128
NF, NPC = FEAT // ROWS, NP // LANES
CH = NF * NPC
AHEAD = 3
EXTRA = 2
NT = (((1,), (1,)), ((), ()))


def split3(v):
    hi = v.astype(BF16)
    rest = v - hi.astype(F32)
    mid = rest.astype(BF16)
    lo = (rest - mid.astype(F32)).astype(BF16)
    return jnp.concatenate([hi, mid, lo], axis=0)


def sum3(v):
    n = v.shape[0] // 3
    return (v[2 * n :] + v[n : 2 * n]) + v[:n]


def row_ones(r, width, value, dtype):
    rows = lax.broadcasted_iota(jnp.int32, (8, width), 0)
    return jnp.where(rows == r, F32(value), F32(0.0)).astype(dtype)


def kernel(*refs):
    (patches, picked_in, text, w_in, w_out, scale_in, bias_in, out) = refs[:8]
    refs = refs[8:]
    picked, scale_ref, bias_ref, send_idx, comp_idx, half_idx, pv, tv, ys, zs, xb, wb, tb, normed, acc, pooled, mean_rows, f1, f2, itl = refs[:20]
    yr = refs[20 : 20 + CH]
    zr = refs[20 + CH : 20 + 2 * CH]
    (lsem, ysend, yrecv, zsend, zrecv, zxsend, zxrecv, xsend, xrecv, wsend, wrecv, dsend, drecv,
     tsend, trecv, f1send, f1recv, f2send, f2recv) = refs[20 + 2 * CH :]

    dp = lax.axis_index("dp")
    mp = lax.axis_index("mp")
    y, h, c = dp // 4, (dp // 2) % 2, dp % 2
    q, x = mp // NX, mp % NX
    z = h * NQ + q
    me = y * NC + c
    yp = (y % 4) * 2 + y // 4

    def ydev(s):
        return (((s // 2) * 2 + h) * 2 + s % 2, mp)

    def zdev(t):
        return ((y * 2 + t // NQ) * 2 + c, (t % NQ) * NX + x)

    def xdev(k):
        return (dp, q * NX + k)

    def core_dev():
        return (y * 4 + h * 2 + 1 - c, mp)

    def remote(src, dst, ssem, rsem, dev):
        return pltpu.make_async_remote_copy(
            src_ref=src, dst_ref=dst, send_sem=ssem, recv_sem=rsem, device_id=dev, device_id_type=MESH)

    def wait(ref, sem):
        pltpu.make_async_copy(ref, ref, sem).wait()

    def load(i, src, dst):
        copy = pltpu.make_async_copy(src, dst, lsem.at[i])
        copy.start()
        return copy

    load_k = load(0, picked_in, picked)
    load_p = load(1, patches, pv)
    load_i = load(2, w_in, wb.at[0, q])
    load_o = load(3, w_out, wb.at[1, q])
    load_t = load(4, text, tv)
    load_s = load(5, scale_in, scale_ref)
    load_b = load(6, bias_in, bias_ref)

    barrier = pltpu.get_barrier_semaphore()

    def greet(dev):
        pl.semaphore_signal(barrier, inc=1, device_id=dev, device_id_type=MESH)

    @pl.loop(1, NS)
    def _(o):
        greet(ydev((me + o) % NS))

    @pl.loop(1, NZ)
    def _(o):
        greet(zdev((z + o) % NZ))

    @pl.loop(1, NX)
    def _(o):
        greet(xdev((x + o) % NX))

    def source_of(v):
        return (v * 4033) >> 19

    base = dp * SUP

    load_k.wait()

    @pl.loop(0, 32)
    def _(n):
        first, second = jnp.int32(0), jnp.int32(0)
        for i in reversed(range(IMG)):
            at = picked[n * IMG + i] - base
            mine = (at >= 0) & (at < SUP)
            second = jnp.where(mine, first, second)
            first = jnp.where(mine, at, first)
        to = (n // 4) * 8 + (n % 2) * 4 + ((n // 2) % 2) * 2
        send_idx[to] = first
        send_idx[to + 1] = second

    def far_first(o, n):
        away = n // 2 - (o + 1) // 2
        return (away * (1 - 2 * (o % 2)) + n) % n

    def gather(k):
        pc, fc = k // NF, k % NF

        @pl.loop(0, NS * 4, unroll=8)
        def _(s):
            image = pv[send_idx[s], fc * ROWS : (fc + 1) * ROWS, pc * LANES : (pc + 1) * LANES]
            ys[k, s // 4, s % 4] = image

        yr[k][pl.ds(me * 4, 4)] = ys[k, me]

    def start_y(k):
        def send(s):
            remote(ys.at[k, s], yr[k].at[pl.ds(me * 4, 4)], ysend.at[k], yrecv.at[k], ydev(s)).start()

        @pl.loop(0, NY - 1)
        def _(o):
            to = (y + far_first(o, NY)) % NY
            send(to * 2 + c)
            send(to * 2 + 1 - c)

        send(me + 1 - 2 * c)

    load_p.wait()
    gather(0)
    pl.semaphore_wait(barrier, NS - 1 + NZ - 1 + NX - 1)
    start_y(0)
    up, down = (z + 1) % NZ, (z + NZ - 1) % NZ

    def qq(k):
        return (q + k + NQ) % NQ

    def w_piece(rnd, way):
        k = qq(-rnd if way == 0 else rnd)
        if rnd == 2:
            return wb.at[c, k, pl.ds(0 if way == 0 else 48, 48)]
        return wb.at[c, k]

    def w_copy(rnd, way):
        piece = w_piece(rnd, way)
        return remote(piece, piece, wsend.at[rnd, way], wrecv.at[rnd, way], zdev(up if way == 0 else down))

    def w_start(rnd):
        w_copy(rnd, 0).start()
        w_copy(rnd, 1).start()

    def w_wait(rnd):
        w_copy(rnd, 0).wait_recv()
        w_copy(rnd, 1).wait_recv()

    def d_copy(j):
        k = (qq(-1), qq(1), qq(-2), qq(2), qq(3))[j]
        return remote(wb.at[c, k], wb.at[c, k], dsend.at[j], drecv.at[j], core_dev())

    gather(1)
    start_y(1)
    load_i.wait()
    load_o.wait()
    w_start(0)
    for k in range(2, AHEAD):
        gather(k)
        start_y(k)

    for e in range(NH):
        sources = []
        for i in range(IMG):
            source = source_of(picked[((y * NH + e) * NC + c) * IMG + i])
            slot = jnp.int32(0)
            for other in sources:
                slot = jnp.where(other == source, 1, slot)
            sources.append(source)
            block = (source // 4) * 8 + (source % 2) * 4 + e * 2 + slot
            to = (e * NQ * 2 + i) if i < IMG - 1 else NZ * 2 + e
            comp_idx[to] = jnp.where((source // 2) % 2 == h, block, 0)
    for r in range(3):
        source = source_of(picked[dp * IMG + (2 * q + r if r < 2 else IMG - 1)])
        half_idx[r] = ((source // 2) % 2) * NQ

    load_t.wait()
    load_s.wait()
    load_b.wait()

    @pl.when(y % 4 == x)
    def _():
        tb[c, h, yp] = jnp.concatenate([tv[...].astype(F32), jnp.zeros((ROWS - IMG, D), F32)], axis=0).astype(BF16)

    def t_spread():
        @pl.when(y % 4 == x)
        def _():
            @pl.loop(0, NY - 1)
            def _(o):
                to = (y + far_first(o, NY)) % NY
                remote(tb.at[c, h, yp], tb.at[c, h, yp], tsend.at[0], trecv.at[y // 4], ((to * 2 + h) * 2 + c, mp)).start()

    def t_mirror():
        piece = tb.at[c, h, pl.ds(2 * x, 2)]
        return remote(piece, piece, tsend.at[1], trecv.at[2], zdev(NZ - 1 - z))

    def t_gather(k):
        piece = tb.at[c, :, pl.ds(2 * x, 2)]
        return remote(piece, piece, tsend.at[2], trecv.at[3 + x], xdev(k))

    def t_core():
        return remote(tb.at[c], tb.at[c], tsend.at[3], trecv.at[7], core_dev())

    def compact(k):
        @pl.loop(0, NZ * 2 + NH, unroll=13)
        def _(g):
            zs[k, g] = yr[k][comp_idx[g]]

        zr[k][z, 0:2] = zs[k, pl.ds(2 * z, 2)]
        zr[k][z, 2] = zs[k, NZ * 2 + h]

    def start_z(k):
        @pl.loop(0, NZ - 1)
        def _(o):
            t = (z + far_first(o, NZ)) % NZ
            remote(zs.at[k, pl.ds(2 * t, 2)], zr[k].at[z, pl.ds(0, 2)], zsend.at[k], zrecv.at[k], zdev(t)).start()

        for e in range(NH):
            t = e * NQ + EXTRA

            @pl.when(z != t)
            def _():
                remote(zs.at[k, pl.ds(NZ * 2 + e, 1)], zr[k].at[z, pl.ds(2, 1)], zxsend.at[k, e], zxrecv.at[k], zdev(t)).start()

    extra = q == EXTRA

    def wait_z(k):
        wait(zr[k].at[pl.ds(0, NZ - 1), pl.ds(0, 2)], zrecv.at[k])

        @pl.when(extra)
        def _():
            wait(zr[k].at[pl.ds(0, NZ - 1), pl.ds(2, 1)], zxrecv.at[k])

    def select(k):
        pc, fc = k // NF, k % NF

        @pl.loop(0, NQ)
        def _(s):
            for r in range(2):
                xb[pc, r, s, x, fc] = zr[k][half_idx[r] + s, r]

        @pl.when(extra)
        def _():
            @pl.loop(0, NQ)
            def _(s):
                xb[pc, 2, s, x, fc] = zr[k][half_idx[2] + s, 2]

    def x_piece(k, r0, n, owner):
        return xb.at[k // NF, pl.ds(r0, n), :, owner, k % NF]

    def x_copy(k, r0, n, owner, to):
        piece = x_piece(k, r0, n, owner)
        i = 0 if r0 == 0 else 1
        return remote(piece, piece, xsend.at[k, i, to], xrecv.at[k, i, owner], xdev(to))

    def start_x(k):
        @pl.loop(1, NX)
        def _(o):
            x_copy(k, 0, 2, x, (x + o) % NX).start()

        @pl.when(extra)
        def _():
            @pl.loop(1, NX)
            def _(o):
                x_copy(k, 2, 1, x, (x + o) % NX).start()

    def wait_x(k):
        @pl.loop(1, NX)
        def _(o):
            owner = (x + o) % NX
            wait(x_piece(k, 0, 2, owner), xrecv.at[k, 0, owner])

        @pl.when(extra)
        def _():
            @pl.loop(1, NX)
            def _(o):
                owner = (x + o) % NX
                wait(x_piece(k, 2, 1, owner), xrecv.at[k, 1, owner])

    def normalize(pc, r):
        flat = xb[pc, r].reshape(D, LANES)
        values = flat.astype(F32)
        center = jnp.sum(values, axis=0, keepdims=True) * F32(1.0 / D)
        values = values - center
        spread = jnp.sum(values * values, axis=0, keepdims=True) * F32(1.0 / D)
        mean = lax.dot_general(row_ones(r, LANES, 1.0 / (NP * NX), BF16), flat, NT, preferred_element_type=F32)
        mean_rows[...] += mean
        return (values * lax.rsqrt(spread + F32(EPS))).astype(BF16)

    def hidden(pc, lanes, first):
        weights = wb[0].reshape(HID, D)
        value = jnp.dot(weights, normed[:, lanes], preferred_element_type=F32)
        value = jax.nn.gelu(value, approximate=True)
        if pc == 0:
            acc[:, lanes] = value
        else:
            acc[:, lanes] += value

    def compute(pc):
        normed[:, 0:LANES] = normalize(pc, 0)
        normed[:, LANES : 2 * LANES] = normalize(pc, 1)
        hidden(pc, slice(0, 2 * LANES), 0)

        @pl.when(extra)
        def _():
            normed[:, 2 * LANES :] = normalize(pc, 2)
            hidden(pc, slice(2 * LANES, 3 * LANES), 2)

    def pool(r):
        total = acc[:, r * LANES : (r + 1) * LANES]
        pooled[...] += lax.dot_general(
            row_ones(r, LANES, 1.0 / NP, F32), total, NT, precision=lax.Precision.HIGHEST, preferred_element_type=F32)

    mean_rows[...] = jnp.zeros((8, D), F32)
    pooled[...] = jnp.zeros((8, HID), F32)

    for k in range(CH):
        wait(yr[k].at[pl.ds(0, (NS - 1) * 4)], yrecv.at[k])
        compact(k)
        start_z(k)
        if k == 1:
            w_wait(0)
            w_start(1)
            d_copy(0).start()
            d_copy(1).start()
        elif k == 2:
            w_wait(1)
            w_start(2)
            d_copy(2).start()
            d_copy(3).start()
        elif k == 3:
            w_wait(2)
            d_copy(4).start()
        if k + AHEAD < CH:
            gather(k + AHEAD)
            start_y(k + AHEAD)
        if k + AHEAD == CH - 1:
            t_spread()
        if k >= 1:
            wait_z(k - 1)
            select(k - 1)
            start_x(k - 1)
    for j in range(2):

        @pl.when(2 * x + j != yp)
        def _():
            wait(tb.at[c, h, 2 * x + j], trecv.at[j])

    t_mirror().start()
    for j in range(5):
        kk = (qq(-1), qq(1), qq(-2), qq(2), qq(3))[j]
        wait(wb.at[1 - c, kk], drecv.at[j])
    for j in range(NF):
        wait_x(j)
    compute(0)
    wait_z(CH - 1)
    select(CH - 1)
    start_x(CH - 1)
    t_mirror().wait_recv()

    @pl.loop(1, NX)
    def _(o):
        t_gather((x + o) % NX).start()

    for j in range(NF, CH):
        wait_x(j)
    compute(1)
    pool(0)
    pool(1)

    @pl.when(extra)
    def _():
        pool(2)

    embed = jnp.dot(pooled[...].astype(BF16), wb[1].reshape(HID, D), preferred_element_type=F32)
    embed = embed + mean_rows[...]
    for r in range(3):
        f1[x, r] = embed[r : r + 1]

    def by_rows(step):
        @pl.when(extra)
        def _():
            step(3)

        @pl.when(q != EXTRA)
        def _():
            step(2)

    def f1_copy(n, to):
        rows = f1.at[x, pl.ds(0, n)]
        return remote(rows, rows, f1send.at[to], f1recv.at[x], xdev(to))

    def f2_copy(n, to):
        rows = f2.at[q, pl.ds(0, n)]
        return remote(rows, rows, f2send.at[to], f2recv.at[q], (dp, to * NX + x))

    @by_rows
    def _(n):
        @pl.loop(1, NX)
        def _(o):
            f1_copy(n, (x + o) % NX).start()

        @pl.loop(1, NX)
        def _(o):
            owner = (x + o) % NX
            wait(tb.at[c, :, pl.ds(2 * owner, 2)], trecv.at[3 + owner])

        t_core().start()

        @pl.loop(1, NX)
        def _(o):
            owner = (x + o) % NX
            wait(f1.at[owner, pl.ds(0, n)], f1recv.at[owner])

        rows = slice(0, n)
        f2[q, rows] = (f1[0, rows] + f1[1, rows]) + (f1[2, rows] + f1[3, rows])

        @pl.loop(1, NQ)
        def _(o):
            f2_copy(n, (q + o) % NQ).start()

    wait(tb.at[1 - c], trecv.at[7])
    squares = tb[...].reshape(NS * NH * ROWS, D).astype(F32)
    squares = squares * squares
    hi = squares.astype(BF16)
    lo = (squares - hi.astype(F32)).astype(BF16)
    ones = jnp.ones((8, D), BF16)
    total = lax.dot_general(ones, lo, NT, preferred_element_type=F32)
    total = total + lax.dot_general(ones, hi, NT, preferred_element_type=F32)
    itl[...] = 1.0 / jnp.sqrt(total + F32(EPS))

    for owner in range(NQ):

        @pl.when(owner != q)
        def _():
            wait(f2.at[owner, pl.ds(0, 3 if owner == EXTRA else 2)], f2recv.at[owner])

    embed = jnp.concatenate(
        [f2[k, r] for k in range(NQ) for r in range(2)] + [f2[EXTRA, 2], jnp.zeros((ROWS - IMG, D), F32)], axis=0)
    length = jnp.sqrt(jnp.sum(embed * embed, axis=1, keepdims=True) + F32(EPS))
    unit = embed / length
    scale = scale_ref[0]
    table = tb[...].reshape(NS * NH * ROWS, D)
    dots = sum3(lax.dot_general(split3(unit), table, NT, preferred_element_type=F32))
    inverse = itl[0:1, :]
    logits = scale * (dots * inverse) + bias_ref[0]
    row = lax.broadcasted_iota(jnp.int32, logits.shape, 0)
    col = lax.broadcasted_iota(jnp.int32, logits.shape, 1)
    label = jnp.where(col == ((c * NH + h) * NY + yp) * ROWS + row, F32(1.0), F32(-1.0))
    slope = -label * jax.nn.sigmoid(-label * logits)
    summed = sum3(jnp.dot(split3(slope * inverse), table, preferred_element_type=F32))
    unit_grad = scale * summed
    along = jnp.sum(unit * unit_grad, axis=1, keepdims=True)
    out[...] = ((unit_grad - unit * along) / length)[0:IMG]

    for k in range(CH):
        wait(yr[k].at[pl.ds(0, (NS - 1) * 4)], ysend.at[k])
        wait(zs.at[k, pl.ds(0, (NZ - 1) * 2)], zsend.at[k])
        for e in range(NH):
            t = e * NQ + EXTRA

            @pl.when(z != t)
            def _():
                wait(zs.at[k, pl.ds(NZ * 2 + e, 1)], zxsend.at[k, e])

        @pl.loop(1, NX)
        def _(o):
            x_copy(k, 0, 2, x, (x + o) % NX).wait_send()

        @pl.when(extra)
        def _():
            @pl.loop(1, NX)
            def _(o):
                x_copy(k, 2, 1, x, (x + o) % NX).wait_send()

    for rnd in range(3):
        w_copy(rnd, 0).wait_send()
        w_copy(rnd, 1).wait_send()
    for j in range(5):
        d_copy(j).wait_send()

    @pl.when(y % 4 == x)
    def _():
        wait(tb.at[c, h, pl.ds(0, NY - 1)], tsend.at[0])

    t_mirror().wait_send()
    wait(tb.at[pl.ds(0, 1), :, pl.ds(0, 6)], tsend.at[2])
    t_core().wait_send()

    @by_rows
    def _(n):
        @pl.loop(1, NX)
        def _(o):
            f1_copy(n, (x + o) % NX).wait_send()

        @pl.loop(1, NQ)
        def _(o):
            f2_copy(n, (q + o) % NQ).wait_send()


def body(patches, picked, text_embed, weight_in, weight_out, logit_scale, logit_bias):
    hbm = pl.BlockSpec(memory_space=pltpu.HBM)
    vmem = pl.BlockSpec(memory_space=pltpu.VMEM)
    dma = pltpu.SemaphoreType.DMA
    return pl.pallas_call(
        kernel,
        out_shape=jax.ShapeDtypeStruct((IMG, D), F32),
        in_specs=[hbm] * 7,
        out_specs=vmem,
        scratch_shapes=[
            pltpu.SMEM((32 * IMG,), jnp.int32),
            pltpu.SMEM((1,), F32),
            pltpu.SMEM((1,), F32),
            pltpu.SMEM((NS * 4,), jnp.int32),
            pltpu.SMEM((NZ * 2 + NH,), jnp.int32),
            pltpu.SMEM((3,), jnp.int32),
            pltpu.VMEM((SUP, FEAT, NP), BF16),
            pltpu.VMEM((IMG, D), BF16),
            pltpu.VMEM((CH, NS, 4, ROWS, LANES), BF16),
            pltpu.VMEM((CH, NZ * 2 + NH, ROWS, LANES), BF16),
            pltpu.VMEM((NPC, 3, NQ, NX, NF, ROWS, LANES), BF16),
            pltpu.VMEM((2, NQ, 96, D), BF16),
            pltpu.VMEM((NC, NH, NY, ROWS, D), BF16),
            pltpu.VMEM((D, 3 * LANES), BF16),
            pltpu.VMEM((HID, 3 * LANES), F32),
            pltpu.VMEM((8, HID), F32),
            pltpu.VMEM((8, D), F32),
            pltpu.VMEM((NX, 3, 1, D), F32),
            pltpu.VMEM((NQ, 3, 1, D), F32),
            pltpu.VMEM((8, NS * NH * ROWS), F32),
        ]
        + [pltpu.VMEM((NS * 4, ROWS, LANES), BF16)] * CH
        + [pltpu.VMEM((NZ, 3, ROWS, LANES), BF16)] * CH
        + [
            dma((7,)), dma((CH,)), dma((CH,)), dma((CH,)), dma((CH,)), dma((CH, NH)), dma((CH,)),
            dma((CH, 2, NX)), dma((CH, 2, NX)), dma((3, 2)), dma((3, 2)), dma((5,)), dma((5,)),
            dma((4,)), dma((8,)), dma((NX,)), dma((NX,)), dma((NQ,)), dma((NQ,)),
        ],
        compiler_params=pltpu.CompilerParams(
            collective_id=0, has_side_effects=True, vmem_limit_bytes=62 * 1024 * 1024),
        cost_estimate=pl.CostEstimate(flops=2_000_000_000, bytes_accessed=5_000_000, transcendentals=1_000_000),
    )(patches, picked, text_embed, weight_in.T, weight_out, logit_scale, logit_bias)


def solution(mesh):
    in_specs = (P("dp", "mp", None), P(), P("dp", None), P(None, "mp"), P("mp", None), P(), P())
    return jax.shard_map(body, mesh=mesh, in_specs=in_specs, out_specs=P("dp", None), check_vma=False)
```

time: 107 us -> 87.9 us (0.82)
  the two profiles are of different devices: /device:TPU:40 before, /device:TPU:56 now
where the time goes in v2:
time: 87.9 us; the launch traced here: 86.9 us
  Pallas kernels  84 us (96%)
  local copies, waits for them, and re-layouts  1.52 us (2%)
  between operations  1.3 us (1%)
    pallas_call x1, Pallas kernels, body(): pl.pallas_call(kernel, out_shape=jax.ShapeDtypeStruct((IMG, D), F32), in_...  84 us

profile of v2, /device:TPU:56, one launch (start us, length us, event | category | flops | bytes accessed | tf_op | source)
XLA Modules:
  0.0 86.9 jit_solution(1391889045392898517)
XLA Ops:
  1.3 84.0 %shard_map.73 = f32[13,1152]{1,0:T(8,128)} custom-call(bf16[130,48,256]{2,1,0:T(8,128)(2,1)} %refs_0_.1, s32[416]{0:T(512)} %refs_1_.1, bf16[13,1152]{1,0:T(8,128)(2,1)} %refs_2_.1, bf16[96,1152]{1,0:T(8,128)(2,1)} %bitcast.1, bf16[96,1152]{1,0:T(8,128)(2,1)} %refs_4_.1, f32[1]{0:T(128)S(6)} %copy.9.refs_5_, f32[1]{0:T(128)S(6)} %copy.10.refs_6_), custom_call_target="tpu_custom_call" | custom-call | flops 2000000000 | bytes 5000000 | tf_op jit(solution)/shard_map/pallas_call | solution.py:538
  85.3 1.5 %copy.11 = f32[13,1152]{1,0:T(8,128)} copy(f32[13,1152]{1,0:T(8,128)} %shard_map.73) | data formatting | bytes 119808

commit v3 on v2

--- a/solution.py
+++ b/solution.py
@@ -152,10 +152,6 @@
 
         send(me + 1 - 2 * c)
 
-    load_p.wait()
-    gather(0)
-    pl.semaphore_wait(barrier, NS - 1 + NZ - 1 + NX - 1)
-    start_y(0)
     up, down = (z + 1) % NZ, (z + NZ - 1) % NZ
 
     def qq(k):
@@ -183,11 +179,15 @@
         k = (qq(-1), qq(1), qq(-2), qq(2), qq(3))[j]
         return remote(wb.at[c, k], wb.at[c, k], dsend.at[j], drecv.at[j], core_dev())
 
-    gather(1)
-    start_y(1)
+    load_p.wait()
+    gather(0)
+    pl.semaphore_wait(barrier, NS - 1 + NZ - 1 + NX - 1)
     load_i.wait()
     load_o.wait()
     w_start(0)
+    start_y(0)
+    gather(1)
+    start_y(1)
     for k in range(2, AHEAD):
         gather(k)
         start_y(k)
@@ -351,17 +351,17 @@
         wait(yr[k].at[pl.ds(0, (NS - 1) * 4)], yrecv.at[k])
         compact(k)
         start_z(k)
-        if k == 1:
+        if k == 0:
             w_wait(0)
             w_start(1)
             d_copy(0).start()
             d_copy(1).start()
-        elif k == 2:
+        elif k == 1:
             w_wait(1)
             w_start(2)
             d_copy(2).start()
             d_copy(3).start()
-        elif k == 3:
+        elif k == 2:
             w_wait(2)
             d_copy(4).start()
         if k + AHEAD < CH:
@@ -369,10 +369,13 @@
             start_y(k + AHEAD)
         if k + AHEAD == CH - 1:
             t_spread()
-        if k >= 1:
-            wait_z(k - 1)
-            select(k - 1)
-            start_x(k - 1)
+        if k >= 2:
+            wait_z(k - 2)
+            select(k - 2)
+            start_x(k - 2)
+    wait_z(CH - 2)
+    select(CH - 2)
+    start_x(CH - 2)
     for j in range(2):
 
         @pl.when(2 * x + j != yp)
@@ -436,13 +439,6 @@
         @pl.loop(1, NX)
         def _(o):
             owner = (x + o) % NX
-            wait(tb.at[c, :, pl.ds(2 * owner, 2)], trecv.at[3 + owner])
-
-        t_core().start()
-
-        @pl.loop(1, NX)
-        def _(o):
-            owner = (x + o) % NX
             wait(f1.at[owner, pl.ds(0, n)], f1recv.at[owner])
 
         rows = slice(0, n)
@@ -452,15 +448,26 @@
         def _(o):
             f2_copy(n, (q + o) % NQ).start()
 
+    @pl.loop(1, NX)
+    def _(o):
+        owner = (x + o) % NX
+        wait(tb.at[c, :, pl.ds(2 * owner, 2)], trecv.at[3 + owner])
+
+    t_core().start()
+
+    def lengths(half):
+        squares = tb[half].reshape(NS * ROWS, D).astype(F32)
+        squares = squares * squares
+        hi = squares.astype(BF16)
+        lo = (squares - hi.astype(F32)).astype(BF16)
+        ones = jnp.ones((8, D), BF16)
+        total = lax.dot_general(ones, lo, NT, preferred_element_type=F32)
+        total = total + lax.dot_general(ones, hi, NT, preferred_element_type=F32)
+        itl[half] = 1.0 / jnp.sqrt(total + F32(EPS))
+
+    lengths(c)
     wait(tb.at[1 - c], trecv.at[7])
-    squares = tb[...].reshape(NS * NH * ROWS, D).astype(F32)
-    squares = squares * squares
-    hi = squares.astype(BF16)
-    lo = (squares - hi.astype(F32)).astype(BF16)
-    ones = jnp.ones((8, D), BF16)
-    total = lax.dot_general(ones, lo, NT, preferred_element_type=F32)
-    total = total + lax.dot_general(ones, hi, NT, preferred_element_type=F32)
-    itl[...] = 1.0 / jnp.sqrt(total + F32(EPS))
+    lengths(1 - c)
 
     for owner in range(NQ):
 
@@ -475,7 +482,7 @@
     scale = scale_ref[0]
     table = tb[...].reshape(NS * NH * ROWS, D)
     dots = sum3(lax.dot_general(split3(unit), table, NT, preferred_element_type=F32))
-    inverse = itl[0:1, :]
+    inverse = jnp.concatenate([itl[0, 0:1], itl[1, 0:1]], axis=1)
     logits = scale * (dots * inverse) + bias_ref[0]
     row = lax.broadcasted_iota(jnp.int32, logits.shape, 0)
     col = lax.broadcasted_iota(jnp.int32, logits.shape, 1)
@@ -560,7 +567,7 @@
             pltpu.VMEM((8, D), F32),
             pltpu.VMEM((NX, 3, 1, D), F32),
             pltpu.VMEM((NQ, 3, 1, D), F32),
-            pltpu.VMEM((8, NS * NH * ROWS), F32),
+            pltpu.VMEM((NC, 8, NS * ROWS), F32),
         ]
         + [pltpu.VMEM((NS * 4, ROWS, LANES), BF16)] * CH
         + [pltpu.VMEM((NZ, 3, ROWS, LANES), BF16)] * CH
@@ -570,7 +577,7 @@
             dma((4,)), dma((8,)), dma((NX,)), dma((NX,)), dma((NQ,)), dma((NQ,)),
         ],
         compiler_params=pltpu.CompilerParams(
-            collective_id=0, has_side_effects=True, vmem_limit_bytes=62 * 1024 * 1024),
+            collective_id=0, has_side_effects=True, vmem_limit_bytes=55000 * 1024),
         cost_estimate=pl.CostEstimate(flops=2_000_000_000, bytes_accessed=5_000_000, transcendentals=1_000_000),
     )(patches, picked, text_embed, weight_in.T, weight_out, logit_scale, logit_bias)
 

time: 87.9 us -> 87.7 us (level)
  Pallas kernels: 84 us -> 83.1 us
    pallas_call x1, Pallas kernels: 84 us -> 83.1 us  [body(): pl.pallas_call(kernel, out_shape=jax.ShapeDtypeStruct((IMG, D), F32), in_...]
    unnamed x1 -> x5, local copies, waits for them, and re-layouts: 1.52 us -> 2.08 us
where the time goes in v3:
time: 87.7 us; the launch traced here: 86.5 us
  Pallas kernels  83.1 us (95%)
  local copies, waits for them, and re-layouts  2.08 us (2%)
  between operations  1.31 us (1%)
    pallas_call x1, Pallas kernels, body(): pl.pallas_call(kernel, out_shape=jax.ShapeDtypeStruct((IMG, D), F32), in_...  83.1 us
    unnamed x5, local copies, waits for them, and re-layouts  2.08 us

profile of v3, /device:TPU:56, one launch (start us, length us, event | category | flops | bytes accessed | tf_op | source)
XLA Modules:
  0.0 86.5 jit_solution(8819769638640433341)
XLA Ops:
  1.3 0.0 copy-start
  1.3 0.8 copy-done
  2.1 0.0 copy-start.1
  2.1 0.7 copy-done.1
  2.7 83.1 %shard_map.73 = f32[13,1152]{1,0:T(8,128)S(1)} custom-call(bf16[130,48,256]{2,1,0:T(8,128)(2,1)} %refs_0_.1, s32[416]{0:T(512)S(1)} %copy-done.1, bf16[13,1152]{1,0:T(8,128)(2,1)S(1)} %copy-done, bf16[96,1152]{1,0:T(8,128)(2,1)} %bitcast.1, bf16[96,1152]{1,0:T(8,128)(2,1)} %refs_4_.1, f32[1]{0:T(128)S(6)} %copy.9.refs_5_, f32[1]{0:T(128)S(6)} %copy.10.refs_6_), custom_call_target="tpu_custom_call" | custom-call | flops 2000000000 | bytes 5000000 | tf_op jit(solution)/shard_map/pallas_call | solution.py:545
  85.9 0.6 copy.11
Async XLA Ops:
  1.3 0.8 copy-start
  2.1 0.7 copy-start.1
